TPU v7x, 128 devices: a whole 4x4x4 slice. The times are simulated.
128 devices in a mesh: head: 4 (over x), seq: 32 (over y, z, core).
Axes of the slice: x: 4, y: 4, z: 4, core: 2. Of those that a mesh axis runs over, the one named last changes fastest.
Arguments:
- queries: bfloat16 [16384, 8192], P('seq', 'head'), may hold values from -200 to 200
- keys: bfloat16 [16384, 8192], P('seq', 'head'), may hold values from -6 to 6
- values: bfloat16 [16384, 8192], P('seq', 'head'), may hold values from -6 to 6
- cotangent: bfloat16 [16384, 8192], P('seq', 'head'), may hold values from -6 to 6
- prefix_keys: bfloat16 [16384, 8192], P('seq', 'head'), may hold values from -1.5 to 1.5
- prefix_values: bfloat16 [16384, 8192], P('seq', 'head'), may hold values from -1.5 to 1.5
- gain: float32 [8192], P('head'), may hold values from 0.5 to 1.5
- lengths: int32 [32], P('seq'), may hold values from 64 to 512, as said below
Outputs:
- normed: bfloat16 [16384, 8192], P('seq', 'head')
- query_grad: bfloat16 [16384, 8192], P('seq', 'head')
- key_grad: bfloat16 [16384, 8192], P('seq', 'head')
- value_grad: bfloat16 [16384, 8192], P('seq', 'head')
- prefix_key_grad: bfloat16 [16384, 8192], P('seq', 'head')
- prefix_value_grad: bfloat16 [16384, 8192], P('seq', 'head')
Inputs may be any that keep to these rules, and one draw needn't show every extreme that they name: `lengths`: one length per response; some response has exactly 512 live slots and some exactly 64.
All inputs are finite; a program needn't handle non-finite values.
Results may differ from a plain program's by a relative error of at most 0.0058.
Values sent between devices are 32-bit elements; how exact they have to be, the bound alone decides.
No kernel may reach another device: no remote copies, remote signals or barrier semaphores. Data moves between devices by JAX's collectives and lax.ppermute only.
A program may use at most 128 MiB of HBM per device.

v0:
```python
import functools
import jax
import jax.numpy as jnp
from jax import lax
from jax.sharding import PartitionSpec as P

H = 64
HEAD_DIM = 128
BLOCK = 256
epsilon = 1e-06


def summed_prefix(partial_state):
    return lax.psum(partial_state, "seq")


def body(queries, keys, values, cotangent, prefix_keys, prefix_values, gain, lengths):
    tok_rows, tok_cols = queries.shape
    heads_here = tok_cols // HEAD_DIM
    block_count = tok_rows // BLOCK
    length = lengths[0]
    is_live = lax.iota(jnp.int32, tok_rows) < length
    live_mask = is_live.astype(jnp.bfloat16)[:, None]
    block_shape = (block_count, BLOCK, heads_here, HEAD_DIM)
    q_live = (queries * live_mask).reshape(block_shape)
    k_live = (keys * live_mask).reshape(block_shape)
    v_live = (values * live_mask).reshape(block_shape)
    causal = (lax.iota(jnp.int32, BLOCK)[:, None] >= lax.iota(jnp.int32, BLOCK)[None, :]).astype(
        jnp.float32
    )
    pre_keys = prefix_keys.reshape(-1, heads_here, HEAD_DIM)
    pre_values = prefix_values.reshape(-1, heads_here, HEAD_DIM)
    partial_state = jnp.einsum(
        "thd,the->hde", pre_keys, pre_values, preferred_element_type=jnp.float32
    )

    def intra_block(index):
        q_block = q_live[index]
        k_block = k_live[index]
        v_block = v_live[index]
        scores = jnp.einsum("bhd,shd->hbs", q_block, k_block, preferred_element_type=jnp.float32)
        scores = (scores * causal).astype(jnp.bfloat16)
        in_block = jnp.einsum("hbs,she->bhe", scores, v_block, preferred_element_type=jnp.float32)
        block_kv = jnp.einsum("bhd,bhe->hde", k_block, v_block, preferred_element_type=jnp.float32)
        return (in_block, scores, block_kv)

    def from_state_of(index, state_bf):
        return jnp.einsum(
            "bhd,hde->bhe", q_live[index], state_bf, preferred_element_type=jnp.float32
        )

    results = []
    score_list = []
    state_list = []
    prefix_state = summed_prefix(partial_state)

    def forward_block(index, state_now):
        state_bf = state_now.astype(jnp.bfloat16)
        in_block, scores, block_kv = intra_block(index)
        return (from_state_of(index, state_bf) + in_block, scores, state_bf, state_now + block_kv)

    state_now = prefix_state
    for index in range(block_count):
        step_fn = functools.partial(forward_block, index)
        packed = step_fn(state_now)
        results.append(packed[0])
        score_list.append(packed[1])
        state_list.append(packed[2])
        state_now = packed[3]
    attended = jnp.concatenate(results, axis=0).reshape(tok_rows, tok_cols)
    scaled_cot = gain * (cotangent * live_mask).astype(jnp.float32)
    square_sum, inner_sum = lax.psum(
        (jnp.sum(attended * attended, axis=1), jnp.sum(scaled_cot * attended, axis=1)), "head"
    )
    root_mean = jnp.sqrt(square_sum / (H * HEAD_DIM) + epsilon)[:, None]
    inner_sum = inner_sum[:, None]
    normed = (gain * attended / root_mean).astype(jnp.bfloat16)
    out_grad = scaled_cot / root_mean - attended * inner_sum / (H * HEAD_DIM * root_mean**3)
    out_grad = out_grad.astype(jnp.bfloat16).reshape(block_shape)

    def backward_block(index, grad_state):
        q_block = q_live[index]
        k_block = k_live[index]
        v_block = v_live[index]
        d_block = out_grad[index]
        scores = score_list[index]
        state_bf = state_list[index]
        grad_bf = grad_state.astype(jnp.bfloat16)
        pscore = jnp.einsum("bhe,she->hbs", d_block, v_block, preferred_element_type=jnp.float32)
        pscore = (pscore * causal).astype(jnp.bfloat16)
        grad_q = jnp.einsum(
            "bhe,hde->bhd", d_block, state_bf, preferred_element_type=jnp.float32
        ) + jnp.einsum("hbs,shd->bhd", pscore, k_block, preferred_element_type=jnp.float32)
        grad_k = jnp.einsum(
            "bhe,hde->bhd", v_block, grad_bf, preferred_element_type=jnp.float32
        ) + jnp.einsum("hbs,bhd->shd", pscore, q_block, preferred_element_type=jnp.float32)
        grad_v = jnp.einsum(
            "bhd,hde->bhe", k_block, grad_bf, preferred_element_type=jnp.float32
        ) + jnp.einsum("hbs,bhe->she", scores, d_block, preferred_element_type=jnp.float32)
        grad_next = grad_state + jnp.einsum(
            "bhd,bhe->hde", q_block, d_block, preferred_element_type=jnp.float32
        )
        return (
            grad_q.astype(jnp.bfloat16),
            grad_k.astype(jnp.bfloat16),
            grad_v.astype(jnp.bfloat16),
            grad_next,
        )

    grad_state = jnp.zeros((heads_here, HEAD_DIM, HEAD_DIM), jnp.float32)
    query_parts = []
    key_parts = []
    value_parts = []
    for index in reversed(range(block_count)):
        step_fn = functools.partial(backward_block, index)
        packed = step_fn(grad_state)
        query_parts.insert(0, packed[0])
        key_parts.insert(0, packed[1])
        value_parts.insert(0, packed[2])
        grad_state = packed[3]
    total_grad = lax.psum(grad_state, "seq")
    wide_keys = pre_keys.astype(jnp.float32)
    wide_values = pre_values.astype(jnp.float32)
    prefix_key_grad = jnp.einsum(
        "the,hde->thd", wide_values, total_grad, precision=lax.Precision.HIGHEST
    )
    prefix_value_grad = jnp.einsum(
        "thd,hde->the", wide_keys, total_grad, precision=lax.Precision.HIGHEST
    )
    query_grad = jnp.concatenate(query_parts, axis=0).reshape(tok_rows, tok_cols)
    key_grad = jnp.concatenate(key_parts, axis=0).reshape(tok_rows, tok_cols)
    value_grad = jnp.concatenate(value_parts, axis=0).reshape(tok_rows, tok_cols)
    return (
        normed,
        query_grad,
        key_grad,
        value_grad,
        prefix_key_grad.astype(jnp.bfloat16).reshape(prefix_keys.shape),
        prefix_value_grad.astype(jnp.bfloat16).reshape(prefix_values.shape),
    )


def solution(mesh):
    return jax.shard_map(
        body,
        mesh=mesh,
        in_specs=(
            P("seq", "head"),
            P("seq", "head"),
            P("seq", "head"),
            P("seq", "head"),
            P("seq", "head"),
            P("seq", "head"),
            P("head"),
            P("seq"),
        ),
        out_specs=(
            P("seq", "head"),
            P("seq", "head"),
            P("seq", "head"),
            P("seq", "head"),
            P("seq", "head"),
            P("seq", "head"),
        ),
        check_vma=False,
    )
```

profile of v0, /device:TPU:1, one launch (start us, length us, event | category | flops | bytes accessed | tf_op | source)
XLA Modules:
  0.0 292.5 jit_solution(10290730926463739367)
XLA Ops:
  7.2 1.5 copy-done
  8.8 3.4 %fusion.8 = f32[16,128,128]{2,1,0:T(8,128)} fusion(bf16[512,2048]{1,0:T(8,128)(2,1)} %param.13, bf16[512,2048]{1,0:T(8,128)(2,1)S(1)} %copy-done), kind=kOutput, calls=%fused_computation.18 | convolution fusion | flops 268435456 | bytes 5242880 | tf_op jit(solution)/shard_map/thd,the->hde/dot_general | solution.py:33
  13.0 3.9 %copy.49 = bf16[512,2048]{0,1:T(8,128)(2,1)} copy(bf16[512,2048]{1,0:T(8,128)(2,1)} %param.8) | data formatting | bytes 4194304 | tf_op args[0]
  16.9 3.9 %copy.53 = bf16[512,2048]{0,1:T(8,128)(2,1)} copy(bf16[512,2048]{1,0:T(8,128)(2,1)} %param.9) | data formatting | bytes 4194304 | tf_op args[1]
  20.8 3.9 %copy.52 = bf16[512,2048]{0,1:T(8,128)(2,1)} copy(bf16[512,2048]{1,0:T(8,128)(2,1)} %param.10) | data formatting | bytes 4194304 | tf_op args[2]
  24.7 3.3 %broadcast_multiply_fusion = (bf16[512,2048]{0,1:T(8,128)(2,1)S(1)}, bf16[512,2048]{0,1:T(8,128)(2,1)S(1)}, bf16[512,2048]{0,1:T(8,128)(2,1)S(1)}) fusion(bf16[512,2048]{0,1:T(8,128)(2,1)} %copy.53, bf16[512]{0:T(512)(128)(2,1)S(1)} %fusion.38, bf16[512,2048]{0,1:T(8,128)(2,1)} %copy.52, bf16[512,2048]{0,1:T(8,128)(2,1)} %copy.49), kind=kLoop, calls=%fused_computation.49 | loop fusion | flops 3145728 | bytes 12583936 | tf_op jit(solution)/shard_map/mul | solution.py:26
  30.8 2.2 fusion.45
  33.0 2.1 multiply_convert_fusion.2
  35.1 3.9 %copy.61 = bf16[512,2048]{0,1:T(8,128)(2,1)} copy(bf16[512,2048]{1,0:T(8,128)(2,1)} %param.11) | data formatting | bytes 4194304 | tf_op args[3]
  39.0 4.1 %fusion.46 = f32[16,128,256]{2,1,0:T(8,128)} fusion(bf16[256,16,128]{0,2,1:T(8,128)(2,1)} %bitcast.148, bf16[16,256,256]{2,1,0:T(8,128)(2,1)} %multiply_convert_fusion.2), kind=kOutput, calls=%fused_computation.72 | convolution fusion | flops 268435456 | bytes 5242880 | tf_op jit(solution)/shard_map/hbs,she->bhe/dot_general | solution.py:43
  43.0 77.5 %all-reduce.4.cloned.1.call-done = f32[16,128,128]{2,1,0:T(8,128)} async-done(((f32[16,128,128]{2,1,0:T(8,128)}), f32[16,128,128]{2,1,0:T(8,128)}) %all-reduce.4.cloned.1.call-update) | async-done | bytes 1048592 | tf_op jit(solution)/shard_map/psum | solution.py:14
  120.5 2.1 fusion.29
  128.5 8.7 %all-reduce = (f32[512]{0:T(512)S(1)}, f32[512]{0:T(512)S(1)}) all-reduce(f32[512]{0:T(512)S(1)} %get-tuple-element.22, f32[512]{0:T(512)S(1)} %fusion.2), channel_id=1, replica_groups=mesh['head'=4,'seq'=32] {'head'}, use_global_device_ids=true, to_apply=%region_2.0 | all-reduce | flops 1024 | bytes 8192 | tf_op jit(solution)/shard_map/psum | solution.py:72
  137.3 4.5 %fusion.5 = (bf16[512,2048]{0,1:T(8,128)(2,1)S(1)}, bf16[512,2048]{0,1:T(8,128)(2,1)}) fusion(f32[512,16,128]{0,2,1:T(8,128)} %copy-done.1, f32[512]{0:T(512)S(1)} %get-tuple-element.32, f32[512]{0:T(512)S(1)} %get-tuple-element.19, f32[512]{0:T(512)S(1)} %get-tuple-element.33, f32[2048]{0:T(1024)S(1)} %copy-done.35, bf16[512,2048]{0,1:T(8,128)(2,1)} %copy.61, ...), kind=kLoop, calls=%fused_computation.9 | loop fusion | flops 11534336 | bytes 10501120 | tf_op jit(solution)/shard_map/convert_element_type | solution.py:79
  141.9 2.2 copy-done.18
  147.4 1.8 fusion.51
  149.1 2.1 fusion.48
  151.3 1.8 fusion.52
  154.3 1.8 fusion.50
  156.1 2.1 fusion.47
  161.1 3.4 %fusion.27 = bf16[256,16,128]{0,2,1:T(8,128)(2,1)} fusion(f32[16,128,256]{2,1,0:T(8,128)} %fusion.52, bf16[256,16,128]{0,2,1:T(8,128)(2,1)S(1)} %bitcast.124, f32[16,128,128]{2,1,0:T(8,128)} %copy-done.19), kind=kOutput, calls=%fused_computation.44 | convolution fusion | flops 135528448 | bytes 5242880 | tf_op jit(solution)/shard_map/bhd,hde->bhe/dot_general | solution.py:97
  164.5 3.6 %fusion.26 = bf16[256,16,128]{0,2,1:T(8,128)(2,1)} fusion(f32[16,128,256]{2,1,0:T(8,128)} %fusion.51, bf16[256,16,128]{0,2,1:T(8,128)(2,1)} %bitcast.149), kind=kOutput, calls=%fused_computation.43 | convolution fusion | flops 135266304 | bytes 4194304 | tf_op jit(solution)/shard_map/bhe,hde->bhd/dot_general | solution.py:94
  174.6 3.9 %copy.82 = bf16[512,2048]{1,0:T(8,128)(2,1)} copy(bf16[512,2048]{0,1:T(8,128)(2,1)} %bitcast.151) | data formatting | bytes 4194304
  178.6 4.0 %copy.80 = bf16[512,2048]{1,0:T(8,128)(2,1)} copy(bf16[512,2048]{0,1:T(8,128)(2,1)} %bitcast.152) | data formatting | bytes 4194304
  182.6 2.4 fusion.25
  186.6 3.9 %copy.81 = bf16[512,2048]{1,0:T(8,128)(2,1)} copy(bf16[512,2048]{0,1:T(8,128)(2,1)} %bitcast.153) | data formatting | bytes 4194304
  190.5 3.9 %copy.79 = bf16[512,2048]{1,0:T(8,128)(2,1)} copy(bf16[512,2048]{0,1:T(8,128)(2,1)} %get-tuple-element.21) | data formatting | bytes 4194304
  194.4 74.1 %all-reduce.6.cloned.1.call-done = f32[16,128,128]{2,1,0:T(8,128)} async-done(((f32[16,128,128]{2,1,0:T(8,128)}), f32[16,128,128]{2,1,0:T(8,128)}) %all-reduce.6.cloned.1.call-update) | async-done | bytes 1048592 | tf_op jit(solution)/shard_map/psum | solution.py:121
  268.5 4.4 %fusion.13 = bf16[16,128,512]{2,1,0:T(8,128)(2,1)} fusion(f32[16,128,128]{2,1,0:T(8,128)} %all-reduce.6.cloned.1.call-done, bf16[512,2048]{1,0:T(8,128)(2,1)S(1)} %copy-done), kind=kOutput, calls=%fused_computation.34 | convolution fusion | flops 1611661312 | bytes 5242880 | tf_op jit(solution)/shard_map/thd,hde->the/dot_general | solution.py:127
  273.0 4.0 %copy.84 = bf16[512,2048]{1,0:T(8,128)(2,1)} copy(bf16[512,2048]{0,1:T(8,128)(2,1)} %bitcast.155) | data formatting | bytes 4194304
  277.0 4.8 %fusion.16 = bf16[16,128,512]{2,1,0:T(8,128)(2,1)} fusion(f32[16,128,128]{2,1,0:T(8,128)S(1)} %copy-done.31, bf16[512,2048]{1,0:T(8,128)(2,1)} %param.13), kind=kOutput, calls=%fused_computation.35 | convolution fusion | flops 1611661312 | bytes 5242880 | tf_op jit(solution)/shard_map/the,hde->thd/dot_general | solution.py:124
  281.7 3.9 %copy.83 = bf16[512,2048]{1,0:T(8,128)(2,1)} copy(bf16[512,2048]{0,1:T(8,128)(2,1)} %bitcast.154) | data formatting | bytes 4194304
  (96 shorter events, 24.3 us)
Async XLA Ops:
  7.2 1.6 copy-start
  7.2 113.3 %all-reduce.4.cloned.1.call-start = ((), (), s32[]{:S(2)}) async-start(), calls=%async_computation | async-start | bytes 2097152 | tf_op jit(solution)/shard_map/psum | solution.py:14
  12.2 256.3 %all-reduce.6.cloned.1.call-start = ((), (), s32[]{:S(2)}) async-start(), calls=%async_computation.1 | async-start | bytes 2097152 | tf_op jit(solution)/shard_map/psum | solution.py:121
  28.1 4.8 %copy-start.20 = (bf16[256,2048]{0,1:T(8,128)(2,1)}, bf16[256,2048]{0,1:T(8,128)(2,1)S(1)}, u32[]{:S(2)}) copy-start(bf16[256,2048]{0,1:T(8,128)(2,1)S(1)} %get-tuple-element.31) | copy-start | bytes 3145732
  29.4 1.4 copy-start.2
  29.4 3.5 %copy-start.9 = (bf16[256,2048]{0,1:T(8,128)(2,1)}, bf16[256,2048]{0,1:T(8,128)(2,1)S(1)}, u32[]{:S(2)}) copy-start(bf16[256,2048]{0,1:T(8,128)(2,1)S(1)} %get-tuple-element.27) | copy-start | bytes 3145732
  30.4 2.5 copy-start.16
  120.5 2.1 copy-start.10
  120.5 2.5 copy-start.28
  123.1 1.4 copy-start.13
  123.1 1.7 copy-start.23
  123.1 2.4 copy-start.25
  126.0 1.7 copy-start.15
  126.0 1.7 copy-start.35
  126.5 2.0 copy-start.1
  141.8 2.3 copy-start.18
  141.9 3.9 %copy-start.7 = (bf16[256,2048]{0,1:T(8,128)(2,1)}, bf16[256,2048]{0,1:T(8,128)(2,1)S(1)}, u32[]{:S(2)}) copy-start(bf16[256,2048]{0,1:T(8,128)(2,1)S(1)} %get-tuple-element.25) | copy-start | bytes 3145732
  141.9 17.7 %copy-start.5 = (bf16[256,2048]{0,1:T(8,128)(2,1)}, bf16[256,2048]{0,1:T(8,128)(2,1)S(1)}, u32[]{:S(2)}) copy-start(bf16[256,2048]{0,1:T(8,128)(2,1)S(1)} %get-tuple-element.24) | copy-start | bytes 3145732
  146.6 13.1 %copy-start.19 = (f32[16,128,128]{2,1,0:T(8,128)}, f32[16,128,128]{2,1,0:T(8,128)S(1)}, u32[]{:S(2)}) copy-start(f32[16,128,128]{2,1,0:T(8,128)S(1)} %fusion.49) | copy-start | bytes 3145732
  147.3 1.8 copy-start.21
  149.1 2.1 copy-start.17
  151.3 1.8 copy-start.3
  164.5 3.6 %copy-start.8 = (bf16[256,2048]{0,1:T(8,128)(2,1)S(1)}, bf16[256,2048]{0,1:T(8,128)(2,1)}, u32[]{:S(2)}) copy-start(bf16[256,2048]{0,1:T(8,128)(2,1)} %copy-done.7) | copy-start | bytes 3145732
  164.5 3.6 %copy-start.26 = (f32[16,128,256]{2,1,0:T(8,128)S(1)}, f32[16,128,256]{2,1,0:T(8,128)}, u32[]{:S(2)}) copy-start(f32[16,128,256]{2,1,0:T(8,128)} %fusion.48) | copy-start | bytes 6291460
  164.5 3.6 %copy-start.30 = (bf16[16,128,128]{2,1,0:T(8,128)(2,1)S(1)}, bf16[16,128,128]{2,1,0:T(8,128)(2,1)}, u32[]{:S(2)}) copy-start(bf16[16,128,128]{2,1,0:T(8,128)(2,1)} %copy-done.29) | copy-start | bytes 1572868
  168.1 1.5 copy-start.34
  169.6 1.5 copy-start.6
  169.6 2.3 copy-start.24
  169.6 3.1 %copy-start.27 = (f32[16,128,256]{2,1,0:T(8,128)S(1)}, f32[16,128,256]{2,1,0:T(8,128)}, u32[]{:S(2)}) copy-start(f32[16,128,256]{2,1,0:T(8,128)} %fusion.47) | copy-start | bytes 6291460
  178.6 4.0 %copy-start.4 = (bf16[256,2048]{0,1:T(8,128)(2,1)S(1)}, bf16[256,2048]{0,1:T(8,128)(2,1)}, u32[]{:S(2)}) copy-start(bf16[256,2048]{0,1:T(8,128)(2,1)} %copy-done.2) | copy-start | bytes 3145732
  182.6 2.5 copy-start.33
  272.9 4.0 %copy-start.31 = (f32[16,128,128]{2,1,0:T(8,128)S(1)}, f32[16,128,128]{2,1,0:T(8,128)}, u32[]{:S(2)}) copy-start(f32[16,128,128]{2,1,0:T(8,128)} %all-reduce.6.cloned.1.call-done) | copy-start | bytes 3145732
  (6 other events, 6.7 us)
Sparse Core Ops, SparseCore 0:
  12.3 108.1 all-reduce.3
  164.6 103.9 all-reduce.5
where the time goes:
time: 294 us; the launch traced here: 292 us
  waiting for transfers between devices  152 us (52%)
  local copies, waits for them, and re-layouts  53.5 us (18%)
  matrix products  50 us (17%)
  between operations  15 us (5%)
  other arithmetic  13.6 us (5%)
  blocking collectives  8.75 us (3%)
    psum x1, waiting for transfers between devices, summed_prefix(): return lax.psum(partial_state, 'seq')  77.5 us
    psum x1, waiting for transfers between devices, body(): total_grad = lax.psum(grad_state, 'seq')  74.1 us
    unnamed x82, local copies, waits for them, and re-layouts  52 us
    psum x1, blocking collectives, body(): lax.psum((jnp.sum(attended * attended, axis=1), jnp.sum(scaled_cot * atte...  8.75 us
    dot_general x2, matrix products, intra_block(): jnp.einsum('hbs,she->bhe', scores, v_block, preferred_element_type=jnp.fl...  6.21 us
    dot_general x2, matrix products, backward_block(): jnp.einsum('bhe,hde->bhd', v_block, grad_bf, preferred_element_type=jnp.f...  6.01 us
  transfers between devices with their start and end apart: 2, of which 2 were waited for; matrix products, arithmetic and copies ran while one was open for 19% of the time, Pallas kernels for 0%

commit v1 on v0

--- a/solution.py
+++ b/solution.py
@@ -118,7 +118,11 @@
         key_parts.insert(0, packed[1])
         value_parts.insert(0, packed[2])
         grad_state = packed[3]
-    total_grad = lax.psum(grad_state, "seq")
+    total_grad = grad_state
+    for hop in (1, 2, 4, 8, 16):
+        total_grad = total_grad + lax.ppermute(
+            total_grad, "seq", [(dev, dev ^ hop) for dev in range(32)]
+        )
     wide_keys = pre_keys.astype(jnp.float32)
     wide_values = pre_values.astype(jnp.float32)
     prefix_key_grad = jnp.einsum(

time: 294 us -> 276 us (0.939)
  waiting for transfers between devices: 152 us -> 129 us
  starting transfers between devices: 0.08 us -> 9.88 us
  matrix products: 50 us -> 40.3 us
  other arithmetic: 13.6 us -> 17.6 us
    psum x1 -> x0, waiting for transfers between devices: 74.1 us -> none  [body(): total_grad = lax.psum(grad_state, 'seq')]
    ppermute x0 -> x5, waiting for transfers between devices: none -> 51.5 us  [body(): lax.ppermute(total_grad, 'seq', [(dev, dev ^ hop) for dev in range(32)])]
    ppermute x0 -> x5, starting transfers between devices: none -> 9.84 us  [body(): lax.ppermute(total_grad, 'seq', [(dev, dev ^ hop) for dev in range(32)])]
    dot_general x2, matrix products: 6.01 us -> 0.85 us  [backward_block(): jnp.einsum('bhe,hde->bhd', v_block, grad_bf, preferred_element_type=jnp.f...]
    add x0 -> x4, other arithmetic: none -> 4.02 us  [body(): total_grad + lax.ppermute(total_grad, 'seq', [(dev, dev ^ hop) for dev in...]
    dot_general x2, matrix products: 4.79 us -> 0.94 us  [backward_block(): jnp.einsum('bhd,hde->bhe', k_block, grad_bf, preferred_element_type=jnp.f...]
    dot_general x2, matrix products: 0.89 us -> 3.85 us  [backward_block(): jnp.einsum('bhe,hde->bhd', d_block, state_bf, preferred_element_type=jnp....]
    unnamed x82 -> x80, local copies, waits for them, and re-layouts: 52 us -> 50.1 us
  transfers between devices with their start and end apart: 2 -> 6, of which waited for: 2 -> 6; matrix products, arithmetic and copies ran while one was open for 19% -> 23% of each run, Pallas kernels for 0% -> 0%
where the time goes in v1:
time: 276 us; the launch traced here: 272 us
  waiting for transfers between devices  129 us (47%)
  local copies, waits for them, and re-layouts  51.7 us (19%)
  matrix products  40.3 us (15%)
  other arithmetic  17.6 us (6%)
  between operations  15.1 us (5%)
  starting transfers between devices  9.88 us (4%)
  blocking collectives  8.56 us (3%)
    psum x1, waiting for transfers between devices, summed_prefix(): return lax.psum(partial_state, 'seq')  77.5 us
    ppermute x5, waiting for transfers between devices, body(): lax.ppermute(total_grad, 'seq', [(dev, dev ^ hop) for dev in range(32)])  51.5 us
    unnamed x80, local copies, waits for them, and re-layouts  50.1 us
    ppermute x5, starting transfers between devices, body(): lax.ppermute(total_grad, 'seq', [(dev, dev ^ hop) for dev in range(32)])  9.84 us
    psum x1, blocking collectives, body(): lax.psum((jnp.sum(attended * attended, axis=1), jnp.sum(scaled_cot * atte...  8.56 us
    dot_general x2, matrix products, intra_block(): jnp.einsum('hbs,she->bhe', scores, v_block, preferred_element_type=jnp.fl...  6.21 us
  transfers between devices with their start and end apart: 6, of which 6 were waited for; matrix products, arithmetic and copies ran while one was open for 23% of the time, Pallas kernels for 0%

profile of v1, /device:TPU:1, one launch (start us, length us, event | category | flops | bytes accessed | tf_op | source)
XLA Modules:
  0.0 272.1 jit_solution(11718967605328679909)
XLA Ops:
  8.8 3.4 %fusion.8 = f32[16,128,128]{2,1,0:T(8,128)} fusion(bf16[512,2048]{1,0:T(8,128)(2,1)S(1)} %copy-done, bf16[512,2048]{1,0:T(8,128)(2,1)} %param.12), kind=kOutput, calls=%fused_computation.18 | convolution fusion | flops 268435456 | bytes 5242880 | tf_op jit(solution)/shard_map/thd,the->hde/dot_general | solution.py:33
  12.9 3.9 %copy.49 = bf16[512,2048]{0,1:T(8,128)(2,1)} copy(bf16[512,2048]{1,0:T(8,128)(2,1)} %param.8) | data formatting | bytes 4194304 | tf_op args[0]
  16.8 3.9 %copy.53 = bf16[512,2048]{0,1:T(8,128)(2,1)} copy(bf16[512,2048]{1,0:T(8,128)(2,1)} %param.9) | data formatting | bytes 4194304 | tf_op args[1]
  20.8 3.9 %copy.52 = bf16[512,2048]{0,1:T(8,128)(2,1)} copy(bf16[512,2048]{1,0:T(8,128)(2,1)} %param.10) | data formatting | bytes 4194304 | tf_op args[2]
  24.7 3.3 %broadcast_multiply_fusion = (bf16[512,2048]{0,1:T(8,128)(2,1)S(1)}, bf16[512,2048]{0,1:T(8,128)(2,1)S(1)}, bf16[512,2048]{0,1:T(8,128)(2,1)S(1)}) fusion(bf16[512,2048]{0,1:T(8,128)(2,1)} %copy.53, bf16[512]{0:T(512)(128)(2,1)S(1)} %fusion.40, bf16[512,2048]{0,1:T(8,128)(2,1)} %copy.52, bf16[512,2048]{0,1:T(8,128)(2,1)} %copy.49), kind=kLoop, calls=%fused_computation.49 | loop fusion | flops 3145728 | bytes 12583936 | tf_op jit(solution)/shard_map/mul | solution.py:26
  30.8 2.2 fusion.47
  33.0 2.1 multiply_convert_fusion.2
  35.0 3.9 %copy.61 = bf16[512,2048]{0,1:T(8,128)(2,1)} copy(bf16[512,2048]{1,0:T(8,128)(2,1)} %param.11) | data formatting | bytes 4194304 | tf_op args[3]
  39.0 4.1 %fusion.48 = f32[16,128,256]{2,1,0:T(8,128)} fusion(bf16[256,16,128]{0,2,1:T(8,128)(2,1)} %bitcast.146, bf16[16,256,256]{2,1,0:T(8,128)(2,1)} %multiply_convert_fusion.2), kind=kOutput, calls=%fused_computation.74 | convolution fusion | flops 268435456 | bytes 5242880 | tf_op jit(solution)/shard_map/hbs,she->bhe/dot_general | solution.py:43
  43.0 77.5 %all-reduce.3.cloned.1.call-done = f32[16,128,128]{2,1,0:T(8,128)} async-done(((f32[16,128,128]{2,1,0:T(8,128)}), f32[16,128,128]{2,1,0:T(8,128)}) %all-reduce.3.cloned.1.call-update) | async-done | bytes 1048592 | tf_op jit(solution)/shard_map/psum | solution.py:14
  120.5 2.1 fusion.29
  128.5 8.6 %all-reduce = (f32[512]{0:T(512)S(1)}, f32[512]{0:T(512)S(1)}) all-reduce(f32[512]{0:T(512)S(1)} %get-tuple-element.22, f32[512]{0:T(512)S(1)} %fusion.2), channel_id=1, replica_groups=mesh['head'=4,'seq'=32] {'head'}, use_global_device_ids=true, to_apply=%region_2.0 | all-reduce | flops 1024 | bytes 8192 | tf_op jit(solution)/shard_map/psum | solution.py:72
  137.1 4.5 %fusion.5 = (bf16[512,2048]{0,1:T(8,128)(2,1)S(1)}, bf16[512,2048]{0,1:T(8,128)(2,1)}) fusion(f32[512,16,128]{0,2,1:T(8,128)} %copy-done.1, f32[512]{0:T(512)S(1)} %get-tuple-element.32, f32[512]{0:T(512)S(1)} %get-tuple-element.19, f32[512]{0:T(512)S(1)} %get-tuple-element.33, f32[2048]{0:T(1024)S(1)} %copy-done.34, bf16[512,2048]{0,1:T(8,128)(2,1)} %copy.61, ...), kind=kLoop, calls=%fused_computation.9 | loop fusion | flops 11534336 | bytes 10501120 | tf_op jit(solution)/shard_map/convert_element_type | solution.py:79
  144.1 2.8 %collective-permute-start = (f32[16,128,128]{2,1,0:T(8,128)S(1)}, f32[16,128,128]{2,1,0:T(8,128)S(1)}, u32[]{:S(2)}, u32[]{:S(2)}) collective-permute-start(f32[16,128,128]{2,1,0:T(8,128)S(1)} %convolution_add_fusion), channel_id=1, source_target_pairs={{0,1},{1,0},{2,3},{3,2},{4,5},{5,4},{6,7},{7,6},{8,9},{9,8},{10,11... | collective-permute-start | bytes 3145736 | tf_op jit(solution)/shard_map/ppermute | solution.py:123
  153.5 19.8 %collective-permute-done.1 = f32[16,128,128]{2,1,0:T(8,128)S(1)} collective-permute-done((f32[16,128,128]{2,1,0:T(8,128)S(1)}, f32[16,128,128]{2,1,0:T(8,128)S(1)}, u32[]{:S(2)}, u32[]{:S(2)}) %collective-permute-start.1) | collective-permute-done | bytes 1048608 | tf_op jit(solution)/shard_map/ppermute | solution.py:123
  173.5 2.7 collective-permute-start.2
  178.3 2.1 fusion.49
  180.4 17.5 %collective-permute-done.2 = f32[16,128,128]{2,1,0:T(8,128)S(1)} collective-permute-done((f32[16,128,128]{2,1,0:T(8,128)S(1)}, f32[16,128,128]{2,1,0:T(8,128)S(1)}, u32[]{:S(2)}, u32[]{:S(2)}) %collective-permute-start.2) | collective-permute-done | bytes 1048608 | tf_op jit(solution)/shard_map/ppermute | solution.py:123
  201.5 4.0 %copy.82 = bf16[512,2048]{1,0:T(8,128)(2,1)} copy(bf16[512,2048]{0,1:T(8,128)(2,1)} %bitcast.151) | data formatting | bytes 4194304
  205.5 2.4 fusion.23
  209.5 4.0 %copy.80 = bf16[512,2048]{1,0:T(8,128)(2,1)} copy(bf16[512,2048]{0,1:T(8,128)(2,1)} %bitcast.152) | data formatting | bytes 4194304
  213.5 2.0 fusion.53
  215.5 5.7 %collective-permute-done.3 = f32[16,128,128]{2,1,0:T(8,128)} collective-permute-done((f32[16,128,128]{2,1,0:T(8,128)}, f32[16,128,128]{2,1,0:T(8,128)}, u32[]{:S(2)}, u32[]{:S(2)}) %collective-permute-start.3) | collective-permute-done | bytes 1048608 | tf_op jit(solution)/shard_map/ppermute | solution.py:123
  221.3 2.7 add.86
  223.9 3.2 %collective-permute-start.4 = (f32[16,128,128]{2,1,0:T(8,128)}, f32[16,128,128]{2,1,0:T(8,128)}, u32[]{:S(2)}, u32[]{:S(2)}) collective-permute-start(f32[16,128,128]{2,1,0:T(8,128)} %add.86), channel_id=1, source_target_pairs={{0,16},{1,17},{2,18},{3,19},{4,20},{5,21},{6,22},{7,23},{8,24},{9,... | collective-permute-start | bytes 3145736 | tf_op jit(solution)/shard_map/ppermute | solution.py:123
  231.1 3.9 %copy.81 = bf16[512,2048]{1,0:T(8,128)(2,1)} copy(bf16[512,2048]{0,1:T(8,128)(2,1)} %bitcast.153) | data formatting | bytes 4194304
  235.0 3.9 %copy.79 = bf16[512,2048]{1,0:T(8,128)(2,1)} copy(bf16[512,2048]{0,1:T(8,128)(2,1)} %get-tuple-element.21) | data formatting | bytes 4194304
  238.9 8.3 %collective-permute-done.4 = f32[16,128,128]{2,1,0:T(8,128)} collective-permute-done((f32[16,128,128]{2,1,0:T(8,128)}, f32[16,128,128]{2,1,0:T(8,128)}, u32[]{:S(2)}, u32[]{:S(2)}) %collective-permute-start.4) | collective-permute-done | bytes 1048608 | tf_op jit(solution)/shard_map/ppermute | solution.py:123
  247.2 4.7 %fusion.16 = bf16[16,128,512]{2,1,0:T(8,128)(2,1)} fusion(f32[16,128,128]{2,1,0:T(8,128)} %add.86, f32[16,128,128]{2,1,0:T(8,128)} %collective-permute-done.4, bf16[512,2048]{1,0:T(8,128)(2,1)S(1)} %copy-done), kind=kOutput, calls=%fused_computation.35 | convolution fusion | flops 1611923456 | bytes 6291456 | tf_op jit(solution)/shard_map/the,hde->thd/dot_general | solution.py:128
  252.0 3.9 %copy.83 = bf16[512,2048]{1,0:T(8,128)(2,1)} copy(bf16[512,2048]{0,1:T(8,128)(2,1)} %bitcast.150) | data formatting | bytes 4194304
  255.9 5.5 %fusion.13 = bf16[16,128,512]{2,1,0:T(8,128)(2,1)} fusion(f32[16,128,128]{2,1,0:T(8,128)} %add.86, f32[16,128,128]{2,1,0:T(8,128)} %collective-permute-done.4, bf16[512,2048]{1,0:T(8,128)(2,1)} %param.12), kind=kOutput, calls=%fused_computation.34 | convolution fusion | flops 1611923456 | bytes 6291456 | tf_op jit(solution)/shard_map/thd,hde->the/dot_general | solution.py:131
  261.4 3.9 %copy.84 = bf16[512,2048]{1,0:T(8,128)(2,1)} copy(bf16[512,2048]{0,1:T(8,128)(2,1)} %bitcast.149) | data formatting | bytes 4194304
  (105 shorter events, 30.6 us)
Async XLA Ops:
  7.2 1.6 copy-start
  7.2 113.4 %all-reduce.3.cloned.1.call-start = ((), (), s32[]{:S(2)}) async-start(), calls=%async_computation | async-start | bytes 2097152 | tf_op jit(solution)/shard_map/psum | solution.py:14
  28.1 4.9 %copy-start.24 = (bf16[256,2048]{0,1:T(8,128)(2,1)}, bf16[256,2048]{0,1:T(8,128)(2,1)S(1)}, u32[]{:S(2)}) copy-start(bf16[256,2048]{0,1:T(8,128)(2,1)S(1)} %get-tuple-element.31) | copy-start | bytes 3145732
  29.5 3.5 %copy-start.7 = (bf16[256,2048]{0,1:T(8,128)(2,1)}, bf16[256,2048]{0,1:T(8,128)(2,1)S(1)}, u32[]{:S(2)}) copy-start(bf16[256,2048]{0,1:T(8,128)(2,1)S(1)} %get-tuple-element.27) | copy-start | bytes 3145732
  30.4 2.5 copy-start.16
  120.5 2.1 copy-start.8
  120.5 2.5 copy-start.30
  123.1 1.7 copy-start.28
  123.1 2.4 copy-start.29
  126.0 1.7 copy-start.15
  126.0 1.7 copy-start.34
  126.6 2.0 copy-start.1
  141.6 1.6 copy-start.9
  141.7 34.4 %copy-start.5 = (bf16[256,2048]{0,1:T(8,128)(2,1)}, bf16[256,2048]{0,1:T(8,128)(2,1)S(1)}, u32[]{:S(2)}) copy-start(bf16[256,2048]{0,1:T(8,128)(2,1)S(1)} %get-tuple-element.24) | copy-start | bytes 3145732
  141.7 1.9 copy-start.13
  143.6 33.3 %copy-start.22 = (f32[16,128,128]{2,1,0:T(8,128)}, f32[16,128,128]{2,1,0:T(8,128)S(1)}, u32[]{:S(2)}) copy-start(f32[16,128,128]{2,1,0:T(8,128)S(1)} %fusion.51) | copy-start | bytes 3145732
  143.7 3.2 %copy-start.26 = (bf16[256,2048]{0,1:T(8,128)(2,1)S(1)}, bf16[256,2048]{0,1:T(8,128)(2,1)}, u32[]{:S(2)}) copy-start(bf16[256,2048]{0,1:T(8,128)(2,1)} %get-tuple-element.37) | copy-start | bytes 3145732
  144.1 3.6 %copy-start.25 = (bf16[256,2048]{0,1:T(8,128)(2,1)S(1)}, bf16[256,2048]{0,1:T(8,128)(2,1)}, u32[]{:S(2)}) copy-start(bf16[256,2048]{0,1:T(8,128)(2,1)} %copy-done.24) | copy-start | bytes 3145732
  144.1 5.0 %collective-permute-start = (f32[16,128,128]{2,1,0:T(8,128)S(1)}, f32[16,128,128]{2,1,0:T(8,128)S(1)}, u32[]{:S(2)}, u32[]{:S(2)}) collective-permute-start(f32[16,128,128]{2,1,0:T(8,128)S(1)} %convolution_add_fusion), channel_id=1, source_target_pairs={{0,1},{1,0},{2,3},{3,2},{4,5},{5,4},{6,7},{7,6},{8,9},{9,8},{10,11... | collective-permute-start | bytes 3145736 | tf_op jit(solution)/shard_map/ppermute | solution.py:123
  149.3 2.2 copy-start.18
  149.3 24.0 %collective-permute-start.1 = (f32[16,128,128]{2,1,0:T(8,128)S(1)}, f32[16,128,128]{2,1,0:T(8,128)S(1)}, u32[]{:S(2)}, u32[]{:S(2)}) collective-permute-start(f32[16,128,128]{2,1,0:T(8,128)S(1)} %add.83), channel_id=1, source_target_pairs={{0,2},{1,3},{2,0},{3,1},{4,6},{5,7},{6,4},{7,5},{8,10},{9,11},{10,... | collective-permute-start | bytes 3145736 | tf_op jit(solution)/shard_map/ppermute | solution.py:123
  151.5 1.6 copy-start.17
  153.5 22.6 %copy-start.3 = (bf16[256,2048]{0,1:T(8,128)(2,1)S(1)}, bf16[256,2048]{0,1:T(8,128)(2,1)}, u32[]{:S(2)}) copy-start(bf16[256,2048]{0,1:T(8,128)(2,1)} %copy-done.2) | copy-start | bytes 3145732
  173.5 24.4 %collective-permute-start.2 = (f32[16,128,128]{2,1,0:T(8,128)S(1)}, f32[16,128,128]{2,1,0:T(8,128)S(1)}, u32[]{:S(2)}, u32[]{:S(2)}) collective-permute-start(f32[16,128,128]{2,1,0:T(8,128)S(1)} %add.84), channel_id=1, source_target_pairs={{0,4},{1,5},{2,6},{3,7},{4,0},{5,1},{6,2},{7,3},{8,12},{9,13},{10,... | collective-permute-start | bytes 3145736 | tf_op jit(solution)/shard_map/ppermute | solution.py:123
  199.0 22.2 %collective-permute-start.3 = (f32[16,128,128]{2,1,0:T(8,128)}, f32[16,128,128]{2,1,0:T(8,128)}, u32[]{:S(2)}, u32[]{:S(2)}) collective-permute-start(f32[16,128,128]{2,1,0:T(8,128)} %add.85), channel_id=1, source_target_pairs={{0,8},{1,9},{2,10},{3,11},{4,12},{5,13},{6,14},{7,15},{8,0},{9,1},... | collective-permute-start | bytes 3145736 | tf_op jit(solution)/shard_map/ppermute | solution.py:123
  201.5 4.0 %copy-start.6 = (bf16[256,2048]{0,1:T(8,128)(2,1)S(1)}, bf16[256,2048]{0,1:T(8,128)(2,1)}, u32[]{:S(2)}) copy-start(bf16[256,2048]{0,1:T(8,128)(2,1)} %copy-done.5) | copy-start | bytes 3145732
  205.5 2.4 copy-start.33
  209.5 4.0 %copy-start.10 = (bf16[256,2048]{0,1:T(8,128)(2,1)S(1)}, bf16[256,2048]{0,1:T(8,128)(2,1)}, u32[]{:S(2)}) copy-start(bf16[256,2048]{0,1:T(8,128)(2,1)} %copy-done.7) | copy-start | bytes 3145732
  215.5 11.6 %copy-start.27 = (bf16[256,2048]{0,1:T(8,128)(2,1)S(1)}, bf16[256,2048]{0,1:T(8,128)(2,1)}, u32[]{:S(2)}) copy-start(bf16[256,2048]{0,1:T(8,128)(2,1)} %get-tuple-element.37) | copy-start | bytes 3145732
  223.9 3.6 %copy-start.14 = (bf16[256,2048]{0,1:T(8,128)(2,1)S(1)}, bf16[256,2048]{0,1:T(8,128)(2,1)}, u32[]{:S(2)}) copy-start(bf16[256,2048]{0,1:T(8,128)(2,1)} %copy-done.11) | copy-start | bytes 3145732
  223.9 3.7 %copy-start.21 = (bf16[16,256,256]{2,1,0:T(8,128)(2,1)S(1)}, bf16[16,256,256]{2,1,0:T(8,128)(2,1)}, u32[]{:S(2)}) copy-start(bf16[16,256,256]{2,1,0:T(8,128)(2,1)} %copy-done.20) | copy-start | bytes 6291460
  223.9 23.3 %collective-permute-start.4 = (f32[16,128,128]{2,1,0:T(8,128)}, f32[16,128,128]{2,1,0:T(8,128)}, u32[]{:S(2)}, u32[]{:S(2)}) collective-permute-start(f32[16,128,128]{2,1,0:T(8,128)} %add.86), channel_id=1, source_target_pairs={{0,16},{1,17},{2,18},{3,19},{4,20},{5,21},{6,22},{7,23},{8,24},{9,... | collective-permute-start | bytes 3145736 | tf_op jit(solution)/shard_map/ppermute | solution.py:123
  (9 other events, 10.9 us)
Sparse Core Ops, SparseCore 0:
  12.4 108.1 all-reduce.2
